TPU v7x, 32 devices: a whole 2x2x4 slice. The times are simulated.
32 devices in a mesh: dom: 8 (over z, y), ka: 4 (over x, core).
Axes of the slice: x: 2, y: 2, z: 4, core: 2. Of those that a mesh axis runs over, the one named last changes fastest.
Arguments:
- density: bfloat16 [64, 16, 64, 64], P('dom', 'ka'), as said below
- columns: int32 [64, 16], replicated, may hold values from 0 to 63, as said below
- live: int32 [64], replicated, may hold values from 1 to 16, as said below
Outputs:
- new_density: bfloat16 [64, 16, 64, 64], P('dom', 'ka')
Inputs may be any that keep to these rules, and one draw needn't show every extreme that they name: columns[i, 0] = i and columns[i, 1] = i - 1 (cyclically over 64); the 16 entries of a block row are distinct and name block rows of domains at most two away from the domain i // 8 of row i, cyclically over the domains. Domains differ in how many of their slots are live. `density`: slot 0 of every block row holds its diagonal block.
All inputs are finite; a program needn't handle non-finite values.
Results may differ from a plain program's by a relative error of at most 0.019.
Values may be sent and summed in bfloat16 or wider, within the bound.
A program may use at most 64 MiB of HBM per device.

v0:
```python
import jax
import jax.numpy as jnp
from jax import lax
from jax.sharding import PartitionSpec as P


def from_behind(value, axis, by):
    count = lax.axis_size(axis)
    return lax.ppermute(value, axis, [(i, (i + by) % count) for i in range(count)])


def shards(density, columns, live):
    rows_here = density.shape[0]
    quarter = density.shape[1]
    slot_count = quarter * lax.axis_size("ka")
    rows_total = columns.shape[0]
    first_row = lax.axis_index("dom") * rows_here
    slot_start = lax.axis_index("ka") * quarter
    full_rows = lax.all_gather(density, "ka", axis=1, tiled=True)
    nearby_rows = []
    for shift_by in (2, 1, -1, -2):
        nearby_rows.append(from_behind(full_rows, "dom", shift_by))
    window = jnp.concatenate(
        [nearby_rows[0], nearby_rows[1], full_rows, nearby_rows[2], nearby_rows[3]], axis=0
    )
    window_start = jnp.mod(first_row - 2 * rows_here, rows_total)
    own_cols = lax.dynamic_slice_in_dim(columns, first_row, rows_here, 0)
    own_live = lax.dynamic_slice_in_dim(live, first_row, rows_here, 0)
    slot_ids = jnp.arange(slot_count, dtype=jnp.int32)
    my_slots = slot_start + jnp.arange(quarter, dtype=jnp.int32)
    valid_mine = (my_slots[None, :] < own_live[:, None])[:, :, None, None]
    group_ids = jnp.arange(quarter, dtype=jnp.int32)

    def contract(left_rows):

        def per_row(row_items):
            left_blocks, row_cols = row_items
            inner_cols = lax.dynamic_slice_in_dim(row_cols, slot_start, quarter, 0)
            inner_local = jnp.mod(inner_cols - window_start, rows_total)
            right_blocks = window[inner_local]
            inner_pattern = columns[inner_cols]
            inner_live = live[inner_cols]
            matches = (inner_pattern[:, None, :] == row_cols[None, :, None]) & (
                slot_ids[None, None, :] < inner_live[:, None, None]
            )
            where_at = jnp.sum(jnp.where(matches, slot_ids[None, None, :], 0), axis=2)
            located = jnp.any(matches, axis=2)
            picked = right_blocks[group_ids[:, None], where_at]
            picked = jnp.where(located[:, :, None, None], picked, jnp.zeros((), picked.dtype))
            return jnp.einsum(
                "tab,tsbc->sac", left_blocks, picked, preferred_element_type=jnp.float32
            )

        return lax.map(per_row, (left_rows, own_cols))

    left_first = jnp.where(valid_mine, density, jnp.zeros((), jnp.bfloat16))
    square_sum = lax.psum_scatter(
        contract(left_first).astype(jnp.bfloat16), "ka", scatter_dimension=1, tiled=True
    ).astype(jnp.float32)
    square_sum = jnp.where(valid_mine, square_sum, jnp.float32(0.0))
    cube_sum = lax.psum_scatter(
        contract(square_sum.astype(jnp.bfloat16)).astype(jnp.bfloat16),
        "ka",
        scatter_dimension=1,
        tiled=True,
    ).astype(jnp.float32)
    cube_sum = jnp.where(valid_mine, cube_sum, jnp.float32(0.0))
    return (3.0 * square_sum - 2.0 * cube_sum).astype(jnp.bfloat16)


def solution(mesh):
    return jax.shard_map(
        shards,
        mesh=mesh,
        in_specs=(P("dom", "ka", None, None), P(), P()),
        out_specs=P("dom", "ka", None, None),
        check_vma=False,
    )
```

profile of v0, /device:TPU:0, one launch (start us, length us, event | category | flops | bytes accessed | tf_op | source)
XLA Modules:
  0.0 463.1 jit_solution(1399467948723805478)
XLA Ops:
  7.3 26.9 %all-gather.2.cloned.1.call-done = bf16[8,16,64,64]{3,2,1,0:T(8,128)(2,1)} async-done(((bf16[8,4,64,64]{3,2,1,0:T(8,128)(2,1)}), bf16[8,16,64,64]{3,2,1,0:T(8,128)(2,1)}) %all-gather.2.cloned.1.call-update) | async-done | bytes 1048592 | tf_op jit(solution)/shard_map/all_gather | solution.py:19
  44.5 40.3 %collective-permute-done = bf16[8,16,64,64]{3,2,1,0:T(8,128)(2,1)} collective-permute-done((bf16[8,16,64,64]{3,2,1,0:T(8,128)(2,1)}, bf16[8,16,64,64]{3,2,1,0:T(8,128)(2,1)}, u32[]{:S(2)}, u32[]{:S(2)}) %collective-permute-start) | collective-permute-done | bytes 1048608 | tf_op jit(solution)/shard_map/ppermute | solution.py:9
  86.6 44.0 %collective-permute-done.1 = bf16[8,16,64,64]{3,2,1,0:T(8,128)(2,1)S(1)} collective-permute-done((bf16[8,16,64,64]{3,2,1,0:T(8,128)(2,1)}, bf16[8,16,64,64]{3,2,1,0:T(8,128)(2,1)S(1)}, u32[]{:S(2)}, u32[]{:S(2)}) %collective-permute-start.1) | collective-permute-done | bytes 1048608 | tf_op jit(solution)/shard_map/ppermute | solution.py:9
  133.3 40.7 %collective-permute-done.3 = bf16[8,16,64,64]{3,2,1,0:T(8,128)(2,1)} collective-permute-done((bf16[8,16,64,64]{3,2,1,0:T(8,128)(2,1)}, bf16[8,16,64,64]{3,2,1,0:T(8,128)(2,1)}, u32[]{:S(2)}, u32[]{:S(2)}) %collective-permute-start.3) | collective-permute-done | bytes 1048608 | tf_op jit(solution)/shard_map/ppermute | solution.py:9
  180.5 84.2 %while.30 = (s32[]{:T(128)}, bf16[8,16,64,64]{3,2,1,0:T(8,128)(2,1)}, s32[8,16]{1,0:T(8,128)S(1)}, s32[]{:T(128)}, s32[64,16]{1,0:T(8,128)S(1)}, /*index=5*/s32[...) while((s32[]{:T(128)}, ...), condition=%wide.region_3.4_spmd.clone.clone, body=%wide.region_0.3_spmd.clone.clone.sunk | while | flops 33826192 | bytes 4535077 | solution.py:54
  182.3 4.7 %gather_fusion = bf16[4,16,64,64]{3,2,1,0:T(8,128)(2,1)S(1)} fusion(bf16[40,16,64,64]{3,2,1,0:T(8,128)(2,1)} %get-tuple-element.754, s32[1024]{0:T(1024)S(1)} %get-tuple-element.708), kind=kCustom, calls=%fused_computation.2.clone.clone.1 | custom fusion | bytes 1048592 | tf_op jit(solution)/shard_map/while/body/eval_jaxpr/gather | solution.py:40
  192.8 4.7 %gather_fusion = bf16[4,16,64,64]{3,2,1,0:T(8,128)(2,1)S(1)} fusion(bf16[40,16,64,64]{3,2,1,0:T(8,128)(2,1)} %get-tuple-element.754, s32[1024]{0:T(1024)S(1)} %get-tuple-element.708), kind=kCustom, calls=%fused_computation.2.clone.clone.1 | custom fusion | bytes 1048592 | tf_op jit(solution)/shard_map/while/body/eval_jaxpr/gather | solution.py:40
  203.4 4.7 %gather_fusion = bf16[4,16,64,64]{3,2,1,0:T(8,128)(2,1)S(1)} fusion(bf16[40,16,64,64]{3,2,1,0:T(8,128)(2,1)} %get-tuple-element.754, s32[1024]{0:T(1024)S(1)} %get-tuple-element.708), kind=kCustom, calls=%fused_computation.2.clone.clone.1 | custom fusion | bytes 1048592 | tf_op jit(solution)/shard_map/while/body/eval_jaxpr/gather | solution.py:40
  213.9 4.7 %gather_fusion = bf16[4,16,64,64]{3,2,1,0:T(8,128)(2,1)S(1)} fusion(bf16[40,16,64,64]{3,2,1,0:T(8,128)(2,1)} %get-tuple-element.754, s32[1024]{0:T(1024)S(1)} %get-tuple-element.708), kind=kCustom, calls=%fused_computation.2.clone.clone.1 | custom fusion | bytes 1048592 | tf_op jit(solution)/shard_map/while/body/eval_jaxpr/gather | solution.py:40
  224.4 4.7 %gather_fusion = bf16[4,16,64,64]{3,2,1,0:T(8,128)(2,1)S(1)} fusion(bf16[40,16,64,64]{3,2,1,0:T(8,128)(2,1)} %get-tuple-element.754, s32[1024]{0:T(1024)S(1)} %get-tuple-element.708), kind=kCustom, calls=%fused_computation.2.clone.clone.1 | custom fusion | bytes 1048592 | tf_op jit(solution)/shard_map/while/body/eval_jaxpr/gather | solution.py:40
  235.0 4.7 %gather_fusion = bf16[4,16,64,64]{3,2,1,0:T(8,128)(2,1)S(1)} fusion(bf16[40,16,64,64]{3,2,1,0:T(8,128)(2,1)} %get-tuple-element.754, s32[1024]{0:T(1024)S(1)} %get-tuple-element.708), kind=kCustom, calls=%fused_computation.2.clone.clone.1 | custom fusion | bytes 1048592 | tf_op jit(solution)/shard_map/while/body/eval_jaxpr/gather | solution.py:40
  245.5 4.7 %gather_fusion = bf16[4,16,64,64]{3,2,1,0:T(8,128)(2,1)S(1)} fusion(bf16[40,16,64,64]{3,2,1,0:T(8,128)(2,1)} %get-tuple-element.754, s32[1024]{0:T(1024)S(1)} %get-tuple-element.708), kind=kCustom, calls=%fused_computation.2.clone.clone.1 | custom fusion | bytes 1048592 | tf_op jit(solution)/shard_map/while/body/eval_jaxpr/gather | solution.py:40
  256.0 4.7 %gather_fusion = bf16[4,16,64,64]{3,2,1,0:T(8,128)(2,1)S(1)} fusion(bf16[40,16,64,64]{3,2,1,0:T(8,128)(2,1)} %get-tuple-element.754, s32[1024]{0:T(1024)S(1)} %get-tuple-element.708), kind=kCustom, calls=%fused_computation.2.clone.clone.1 | custom fusion | bytes 1048592 | tf_op jit(solution)/shard_map/while/body/eval_jaxpr/gather | solution.py:40
  266.6 47.9 %all-reduce.5.cloned.1.call-done = bf16[8,16,64,64]{3,2,1,0:T(8,128)(2,1)} async-done(((bf16[8,16,64,64]{3,2,1,0:T(8,128)(2,1)}), bf16[8,16,64,64]{3,2,1,0:T(8,128)(2,1)}) %all-reduce.5.cloned.1.call-update) | async-done | bytes 1048592
  318.4 84.2 %while.31 = (s32[]{:T(128)}, bf16[8,16,64,64]{3,2,1,0:T(8,128)(2,1)}, s32[8,16]{1,0:T(8,128)S(1)}, s32[]{:T(128)}, s32[64,16]{1,0:T(8,128)S(1)}, /*index=5*/s32[...) while((s32[]{:T(128)}, ...), condition=%wide.region_8.9_spmd.clone.clone, body=%wide.region_5.8_spmd.clone.clone.sunk | while | flops 33826192 | bytes 4535077 | solution.py:54
  320.2 4.7 %gather_fusion.4 = bf16[4,16,64,64]{3,2,1,0:T(8,128)(2,1)S(1)} fusion(bf16[40,16,64,64]{3,2,1,0:T(8,128)(2,1)} %get-tuple-element.790, s32[1024]{0:T(1024)S(1)} %get-tuple-element.721), kind=kCustom, calls=%fused_computation.6.clone.clone.1 | custom fusion | bytes 1048592 | tf_op jit(solution)/shard_map/while/body/eval_jaxpr/gather | solution.py:40
  330.7 4.7 %gather_fusion.4 = bf16[4,16,64,64]{3,2,1,0:T(8,128)(2,1)S(1)} fusion(bf16[40,16,64,64]{3,2,1,0:T(8,128)(2,1)} %get-tuple-element.790, s32[1024]{0:T(1024)S(1)} %get-tuple-element.721), kind=kCustom, calls=%fused_computation.6.clone.clone.1 | custom fusion | bytes 1048592 | tf_op jit(solution)/shard_map/while/body/eval_jaxpr/gather | solution.py:40
  341.2 4.7 %gather_fusion.4 = bf16[4,16,64,64]{3,2,1,0:T(8,128)(2,1)S(1)} fusion(bf16[40,16,64,64]{3,2,1,0:T(8,128)(2,1)} %get-tuple-element.790, s32[1024]{0:T(1024)S(1)} %get-tuple-element.721), kind=kCustom, calls=%fused_computation.6.clone.clone.1 | custom fusion | bytes 1048592 | tf_op jit(solution)/shard_map/while/body/eval_jaxpr/gather | solution.py:40
  351.8 4.7 %gather_fusion.4 = bf16[4,16,64,64]{3,2,1,0:T(8,128)(2,1)S(1)} fusion(bf16[40,16,64,64]{3,2,1,0:T(8,128)(2,1)} %get-tuple-element.790, s32[1024]{0:T(1024)S(1)} %get-tuple-element.721), kind=kCustom, calls=%fused_computation.6.clone.clone.1 | custom fusion | bytes 1048592 | tf_op jit(solution)/shard_map/while/body/eval_jaxpr/gather | solution.py:40
  362.3 4.7 %gather_fusion.4 = bf16[4,16,64,64]{3,2,1,0:T(8,128)(2,1)S(1)} fusion(bf16[40,16,64,64]{3,2,1,0:T(8,128)(2,1)} %get-tuple-element.790, s32[1024]{0:T(1024)S(1)} %get-tuple-element.721), kind=kCustom, calls=%fused_computation.6.clone.clone.1 | custom fusion | bytes 1048592 | tf_op jit(solution)/shard_map/while/body/eval_jaxpr/gather | solution.py:40
  372.8 4.7 %gather_fusion.4 = bf16[4,16,64,64]{3,2,1,0:T(8,128)(2,1)S(1)} fusion(bf16[40,16,64,64]{3,2,1,0:T(8,128)(2,1)} %get-tuple-element.790, s32[1024]{0:T(1024)S(1)} %get-tuple-element.721), kind=kCustom, calls=%fused_computation.6.clone.clone.1 | custom fusion | bytes 1048592 | tf_op jit(solution)/shard_map/while/body/eval_jaxpr/gather | solution.py:40
  383.3 4.7 %gather_fusion.4 = bf16[4,16,64,64]{3,2,1,0:T(8,128)(2,1)S(1)} fusion(bf16[40,16,64,64]{3,2,1,0:T(8,128)(2,1)} %get-tuple-element.790, s32[1024]{0:T(1024)S(1)} %get-tuple-element.721), kind=kCustom, calls=%fused_computation.6.clone.clone.1 | custom fusion | bytes 1048592 | tf_op jit(solution)/shard_map/while/body/eval_jaxpr/gather | solution.py:40
  393.8 4.7 %gather_fusion.4 = bf16[4,16,64,64]{3,2,1,0:T(8,128)(2,1)S(1)} fusion(bf16[40,16,64,64]{3,2,1,0:T(8,128)(2,1)} %get-tuple-element.790, s32[1024]{0:T(1024)S(1)} %get-tuple-element.721), kind=kCustom, calls=%fused_computation.6.clone.clone.1 | custom fusion | bytes 1048592 | tf_op jit(solution)/shard_map/while/body/eval_jaxpr/gather | solution.py:40
  402.6 51.6 %all-reduce.7.cloned.1.call-done = bf16[8,16,64,64]{3,2,1,0:T(8,128)(2,1)} async-done(((bf16[8,16,64,64]{3,2,1,0:T(8,128)(2,1)}), bf16[8,16,64,64]{3,2,1,0:T(8,128)(2,1)}) %all-reduce.7.cloned.1.call-update) | async-done | bytes 1048592
  (307 shorter events, 121.3 us)
Async XLA Ops:
  6.5 27.7 %all-gather.2.cloned.1.call-start = ((), (), s32[]{:S(2)}) async-start(), calls=%async_computation | async-start | bytes 2621440 | tf_op jit(solution)/shard_map/all_gather | solution.py:19
  7.3 307.3 %all-reduce.5.cloned.1.call-start = ((), (), s32[]{:S(2)}) async-start(), calls=%async_computation.1 | async-start | bytes 4194304
  34.2 50.6 %collective-permute-start = (bf16[8,16,64,64]{3,2,1,0:T(8,128)(2,1)}, bf16[8,16,64,64]{3,2,1,0:T(8,128)(2,1)}, u32[]{:S(2)}, u32[]{:S(2)}) collective-permute-start(bf16[8,16,64,64]{3,2,1,0:T(8,128)(2,1)} %all-gather.2.cloned.1.call-done), channel_id=1, source_target_pairs={{0,8},{4,12},{8,16},{12,20},{16,24},{20,28},{24,0},{28,4},{1,9},{5... | collective-permute-start | bytes 3145736 | tf_op jit(solution)/shard_map/ppermute | solution.py:9
  35.7 94.9 %collective-permute-start.1 = (bf16[8,16,64,64]{3,2,1,0:T(8,128)(2,1)}, bf16[8,16,64,64]{3,2,1,0:T(8,128)(2,1)S(1)}, u32[]{:S(2)}, u32[]{:S(2)}) collective-permute-start(bf16[8,16,64,64]{3,2,1,0:T(8,128)(2,1)} %all-gather.2.cloned.1.call-done), channel_id=1, source_target_pairs={{0,4},{4,8},{8,12},{12,16},{16,20},{20,24},{24,28},{28,0},{1,5},{5... | collective-permute-start | bytes 3145736 | tf_op jit(solution)/shard_map/ppermute | solution.py:9
  37.9 93.5 %collective-permute-start.2 = (bf16[8,16,64,64]{3,2,1,0:T(8,128)(2,1)}, bf16[8,16,64,64]{3,2,1,0:T(8,128)(2,1)}, u32[]{:S(2)}, u32[]{:S(2)}) collective-permute-start(bf16[8,16,64,64]{3,2,1,0:T(8,128)(2,1)} %all-gather.2.cloned.1.call-done), channel_id=1, source_target_pairs={{0,28},{4,0},{8,4},{12,8},{16,12},{20,16},{24,20},{28,24},{1,29},{... | collective-permute-start | bytes 3145736 | tf_op jit(solution)/shard_map/ppermute | solution.py:9
  41.2 132.8 %collective-permute-start.3 = (bf16[8,16,64,64]{3,2,1,0:T(8,128)(2,1)}, bf16[8,16,64,64]{3,2,1,0:T(8,128)(2,1)}, u32[]{:S(2)}, u32[]{:S(2)}) collective-permute-start(bf16[8,16,64,64]{3,2,1,0:T(8,128)(2,1)} %all-gather.2.cloned.1.call-done), channel_id=1, source_target_pairs={{0,24},{4,28},{8,0},{12,4},{16,8},{20,12},{24,16},{28,20},{1,25},{... | collective-permute-start | bytes 3145736 | tf_op jit(solution)/shard_map/ppermute | solution.py:9
  86.6 44.5 %copy-start.2 = (bf16[8,16,64,64]{3,2,1,0:T(8,128)(2,1)S(1)}, bf16[8,16,64,64]{3,2,1,0:T(8,128)(2,1)}, u32[]{:S(2)}) copy-start(bf16[8,16,64,64]{3,2,1,0:T(8,128)(2,1)} %all-gather.2.cloned.1.call-done) | copy-start | bytes 3145732
  175.9 4.6 copy-start.1
  175.9 4.6 copy-start
  264.7 0.7 copy-start.3
  264.7 189.5 %all-reduce.7.cloned.1.call-start = ((), (), s32[]{:S(2)}) async-start(), calls=%async_computation.2 | async-start | bytes 4194304
Sparse Core Ops, SparseCore 0:
  8.9 25.2 all-gather.1
  264.9 49.6 all-reduce.4
  402.7 51.4 all-reduce.6
where the time goes:
time: 465 us; the launch traced here: 463 us
  waiting for transfers between devices  252 us (54%)
  local copies, waits for them, and re-layouts  151 us (32%)
  matrix products  21.1 us (5%)
  other arithmetic  17.2 us (4%)
  between operations  13.8 us (3%)
  starting transfers between devices  6.83 us (1%)
    ppermute x4, waiting for transfers between devices, from_behind(): lax.ppermute(value, axis, [(i, (i + by) % count) for i in range(count)])  125 us
    unnamed x5, waiting for transfers between devices  100 us
    gather x16, local copies, waits for them, and re-layouts, per_row(): right_blocks = window[inner_local]  75.6 us
    all_gather x1, waiting for transfers between devices, shards(): full_rows = lax.all_gather(density, 'ka', axis=1, tiled=True)  26.9 us
    gather x32, local copies, waits for them, and re-layouts, per_row(): picked = right_blocks[group_ids[:, None], where_at]  23.3 us
    dot_general x16, matrix products, per_row(): jnp.einsum('tab,tsbc->sac', left_blocks, picked, preferred_element_type=j...  21.1 us
    dynamic_update_slice x32, local copies, waits for them, and re-layouts, contract(): return lax.map(per_row, (left_rows, own_cols))  14.5 us
    gather x16, local copies, waits for them, and re-layouts, per_row(): inner_live = live[inner_cols]  10.2 us
  transfers between devices with their start and end apart: 7, of which 6 were waited for; matrix products, arithmetic and copies ran while one was open for 2% of the time, Pallas kernels for 0%

commit v1 on v0

v1 whole, which is shorter than its diff:
```python
import functools

import jax
import jax.numpy as jnp
from jax import lax
from jax.experimental import pallas as pl
from jax.experimental.pallas import tpu as pltpu
from jax.sharding import PartitionSpec as P

MESH = pl.DeviceIdType.MESH
BF = jnp.bfloat16
F32 = jnp.float32
REACH = (0, 1, -1, 2, -2)


def iota(shape, dim):
    return lax.broadcasted_iota(jnp.int32, shape, dim)


def dot(a, b):
    return jnp.dot(a, b, preferred_element_type=F32)


def exact_dot(a, b):
    return dot(a, b).astype(BF)


def onehot(cond):
    return jnp.where(cond, F32(1), F32(0)).astype(BF)


def permutation(source, target):
    sizes = {"h": 2, "k": 4, "u": 4}
    lane = iota((512, 1), 0)
    digits, rest = {}, lane // 16
    for name in reversed(source):
        digits[name] = rest % sizes[name]
        rest = rest // sizes[name]
    place = jnp.zeros_like(lane)
    for name in target:
        place = place * sizes[name] + digits[name]
    place = place * 16 + lane % 16
    return onehot(jnp.broadcast_to(place, (512, 512)) == iota((512, 512), 1))


def kernel(
    ndom, rows_total, live_ref, density_ref, columns_ref, out_ref,
    a_buf, pieces, zin, win, left_in, square_in, square_own, new_pieces, yin,
    expand, gather, ldense, ddense, total, square_f32, mask_buf, rel_buf,
    send_a, recv_a, send_w, recv_w, send_l, recv_l, send_s, recv_s, send_n, recv_n,
):
    dom, ka = lax.axis_index("dom"), lax.axis_index("ka")

    def near(shift):
        return lax.rem(dom + shift + ndom, ndom)

    def peer(shift):
        return lax.rem(ka + shift, 4)

    barrier = pltpu.get_barrier_semaphore()
    for shift in REACH[1:]:
        pl.semaphore_signal(barrier, inc=1, device_id=(near(shift), ka), device_id_type=MESH)
    for shift in (1, 2, 3):
        pl.semaphore_signal(barrier, inc=1, device_id=(dom, peer(shift)), device_id_type=MESH)

    for i in range(4):
        for h in range(2):
            for u in range(4):
                at = (h * 4 + u) * 64
                a_buf[i * 64:(i + 1) * 64, at:at + 64] = density_ref[h * 4 + i, u]
    packed = exact_dot(a_buf[...], permutation("huk", "khu"))
    for k in range(4):
        pieces[k] = packed[:, k * 128:(k + 1) * 128]
    zin[ka] = pieces[ka]

    pl.semaphore_wait(barrier, 7)

    def spread(src_of, dst, send, recv):
        copies = []
        for shift in (2, 3, 1):
            to = peer(shift)
            copies.append(pltpu.make_async_remote_copy(
                src_ref=src_of(to), dst_ref=dst.at[ka],
                send_sem=send.at[shift - 1], recv_sem=recv.at[shift - 1],
                device_id=(dom, to), device_id_type=MESH))
        for copy in copies:
            copy.start()
        return copies

    copies_a = spread(lambda to: pieces.at[to], zin, send_a, recv_a)

    first_row = lax.rem((dom - 2 + ndom) * 8, rows_total)
    slot = iota((8, 16), 1)
    for o in range(5):
        base = pl.multiple_of(near(o - 2) * 8, 8)
        cols = columns_ref[pl.ds(base, 8), :]
        rel = cols - first_row
        rel = jnp.where(rel < 0, rel + rows_total, rel)
        row = iota((8, 16), 0)
        count = jnp.zeros((8, 16), jnp.int32)
        for r in range(8):
            count = jnp.where(row == r, live_ref[base + r], count)
        keep = (slot < count) & (rel < 40)
        rel_buf[o * 8:(o + 1) * 8, :] = jnp.where(keep, rel, -64).astype(F32)
    rel_all = rel_buf[...].astype(BF)
    repeat = onehot(iota((256, 16), 0) // 16 == iota((256, 16), 1))
    target = lax.dot_general(repeat, rel_all, (((1,), (1,)), ((), ())), preferred_element_type=F32)
    target = target * 16.0 + (iota((256, 40), 0) % 16).astype(F32)
    target_own = lax.dot_general(rel_all[16:24], repeat, (((1,), (1,)), ((), ())), preferred_element_type=F32)
    target_own = target_own * 16.0 + (iota((8, 256), 1) % 16).astype(F32)

    def build(o):
        lane = iota((256, 640), 1).astype(F32)
        for r in range(8):
            n = o * 8 + r
            expand[n] = onehot(jnp.broadcast_to(target[:, n:n + 1], (256, 640)) == lane)

    build(2)
    place = iota((640, 256), 0).astype(F32)
    for r in range(8):
        gather[r] = onehot(jnp.broadcast_to(target_own[r:r + 1, :], (640, 256)) == place)

    for copy in copies_a:
        copy.wait_recv()
    z = jnp.concatenate([zin[k] for k in range(4)], axis=1)
    mine = exact_dot(z, permutation("khu", "hku"))
    win[2, 0:256, :] = mine[:, 0:256]
    win[2, 256:512, :] = mine[:, 256:512]
    left_in[ka] = win[2]

    copies_w = {}
    for n, shift in enumerate((2, -2, 1, -1)):
        copies_w[shift] = pltpu.make_async_remote_copy(
            src_ref=win.at[2], dst_ref=win.at[2 - shift],
            send_sem=send_w.at[n], recv_sem=recv_w.at[n],
            device_id=(near(shift), ka), device_id_type=MESH)
        copies_w[shift].start()
    copies_l = spread(lambda to: win.at[2], left_in, send_l, recv_l)

    for o in (0, 1, 3, 4):
        build(o)
    for r in range(8):
        hit = jnp.max(expand[16 + r].astype(F32), axis=0, keepdims=True)
        mask_buf[r:r + 1, :] = hit

    def expand_window(o):
        def step(r, _):
            d = exact_dot(win[o, pl.ds(pl.multiple_of(r * 64, 64), 64), :], expand[o * 8 + r])
            for k in range(4):
                at = pl.multiple_of(o * 512 + k * 128 + r * 16, 16)
                ddense[pl.ds(at, 16), :] = d[k * 16:(k + 1) * 16, :]
            return 0
        lax.fori_loop(0, 8, step, 0)

    def expand_left(src):
        def step(r, _):
            rows = pl.ds(pl.multiple_of(r * 64, 64), 64)
            x = jnp.concatenate([src[k, rows, :] for k in range(4)], axis=0)
            d = exact_dot(x, expand[16 + r])
            for k in range(4):
                for o in range(5):
                    ldense[rows, o * 512 + k * 128:o * 512 + (k + 1) * 128] = (
                        d[k * 64:(k + 1) * 64, o * 128:(o + 1) * 128])
            return 0
        lax.fori_loop(0, 8, step, 0)

    expand_window(2)
    for copy in copies_l:
        copy.wait_recv()
    expand_left(left_in)
    square_f32[...] = dot(ldense[:, 1024:1536], ddense[1024:1536, :])
    for shift in (1, -1, 2, -2):
        o = 2 - shift
        copies_w[shift].wait_recv()
        expand_window(o)
        square_f32[...] += dot(ldense[:, o * 512:(o + 1) * 512], ddense[o * 512:(o + 1) * 512, :])

    def pick(value, r):
        kept = jnp.where(mask_buf[pl.ds(r, 1), :] > 0.5, value, F32(0))
        return exact_dot(kept.astype(BF), gather[r])

    for r in range(8):
        rows = slice(r * 64, (r + 1) * 64)
        square_own[rows, :] = pick(square_f32[rows, :], r)
    square_in[ka] = square_own[...]
    copies_s = spread(lambda to: square_own, square_in, send_s, recv_s)
    for copy in copies_s:
        copy.wait_recv()
    expand_left(square_in)
    total[...] = 3.0 * square_f32[...] - 2.0 * dot(ldense[...], ddense[...])
    news = []
    for r in range(8):
        news.append(pick(total[r * 64:(r + 1) * 64, :], r))
    new = jnp.concatenate(
        [jnp.concatenate(news[:4], axis=0), jnp.concatenate(news[4:], axis=0)], axis=1)
    packed = exact_dot(new, permutation("hku", "khu"))
    for k in range(4):
        new_pieces[k] = packed[:, k * 128:(k + 1) * 128]
    yin[ka] = new_pieces[ka]
    copies_n = spread(lambda to: new_pieces.at[to], yin, send_n, recv_n)
    back = permutation("khu", "huk")
    for copy in copies_n:
        copy.wait_recv()
    y = exact_dot(jnp.concatenate([yin[k] for k in range(4)], axis=1), back)
    for i in range(4):
        for h in range(2):
            for u in range(4):
                at = (h * 4 + u) * 64
                out_ref[h * 4 + i, u] = y[i * 64:(i + 1) * 64, at:at + 64]
    for copies in (copies_a, copies_l, copies_s, copies_n, list(copies_w.values())):
        for copy in copies:
            copy.wait_send()


def shards(density, columns, live):
    rows_total = columns.shape[0]
    dma = pltpu.SemaphoreType.DMA
    vmem = pltpu.VMEM
    return pl.pallas_call(
        functools.partial(kernel, lax.axis_size("dom"), rows_total),
        out_shape=jax.ShapeDtypeStruct(density.shape, BF),
        in_specs=[
            pl.BlockSpec(memory_space=pltpu.SMEM),
            pl.BlockSpec(memory_space=pltpu.VMEM),
            pl.BlockSpec(memory_space=pltpu.VMEM),
        ],
        out_specs=pl.BlockSpec(memory_space=pltpu.VMEM),
        scratch_shapes=[
            vmem((256, 512), BF),
            vmem((4, 256, 128), BF),
            vmem((4, 256, 128), BF),
            vmem((5, 512, 256), BF),
            vmem((4, 512, 256), BF),
            vmem((4, 512, 256), BF),
            vmem((512, 256), BF),
            vmem((4, 256, 128), BF),
            vmem((4, 256, 128), BF),
            vmem((40, 256, 640), BF),
            vmem((8, 640, 256), BF),
            vmem((512, 2560), BF),
            vmem((2560, 640), BF),
            vmem((512, 640), F32),
            vmem((512, 640), F32),
            vmem((8, 640), F32),
            vmem((40, 16), F32),
            dma((3,)), dma((3,)), dma((4,)), dma((4,)), dma((3,)), dma((3,)),
            dma((3,)), dma((3,)), dma((3,)), dma((3,)),
        ],
        compiler_params=pltpu.CompilerParams(
            collective_id=0, has_side_effects=True, vmem_limit_bytes=56 * 1024 * 1024),
    )(live, density, columns)


def solution(mesh):
    return jax.shard_map(
        shards,
        mesh=mesh,
        in_specs=(P("dom", "ka", None, None), P(), P()),
        out_specs=P("dom", "ka", None, None),
        check_vma=False,
    )
```

time: 465 us -> 68.3 us (0.15)
  waiting for transfers between devices: 252 us -> 0 us
  local copies, waits for them, and re-layouts: 151 us -> 3.26 us
  Pallas kernels: 0 us -> 64.8 us
  matrix products: 21.1 us -> 0 us
  other arithmetic: 17.2 us -> 0 us
  between operations: 13.8 us -> 0.01 us
  starting transfers between devices: 6.83 us -> 0 us
    ppermute x4 -> x0, waiting for transfers between devices: 125 us -> none  [from_behind(): lax.ppermute(value, axis, [(i, (i + by) % count) for i in range(count)])]
    gather x80 -> x0, local copies, waits for them, and re-layouts: 118 us -> none  [the longest x16 75.6 us: per_row(): right_blocks = window[inner_local]]
    unnamed x5 -> x0, waiting for transfers between devices: 100 us -> none
    pallas_call x0 -> x1, Pallas kernels: none -> 64.8 us  [shards(): pl.pallas_call(functools.partial(kernel, lax.axis_size('dom'), rows_total...]
    all_gather x1 -> x0, waiting for transfers between devices: 26.9 us -> none  [shards(): full_rows = lax.all_gather(density, 'ka', axis=1, tiled=True)]
    dot_general x16 -> x0, matrix products: 21.1 us -> none  [per_row(): jnp.einsum('tab,tsbc->sac', left_blocks, picked, preferred_element_type=j...]
    dynamic_update_slice x32 -> x0, local copies, waits for them, and re-layouts: 14.5 us -> none  [contract(): return lax.map(per_row, (left_rows, own_cols))]
    ppermute x4 -> x0, starting transfers between devices: 6.75 us -> none  [from_behind(): lax.ppermute(value, axis, [(i, (i + by) % count) for i in range(count)])]
  transfers between devices with their start and end apart: 7 -> 0, of which waited for: 6 -> 0; matrix products, arithmetic and copies ran while one was open for 2% -> 0% of each run, Pallas kernels for 0% -> 0%
where the time goes in v1:
time: 68.3 us; the launch traced here: 68.1 us
  Pallas kernels  64.8 us (95%)
  local copies, waits for them, and re-layouts  3.26 us (5%)
    pallas_call x1, Pallas kernels, shards(): pl.pallas_call(functools.partial(kernel, lax.axis_size('dom'), rows_total...  64.8 us
    unnamed x2, local copies, waits for them, and re-layouts  3.26 us

profile of v1, /device:TPU:0, one launch (start us, length us, event | category | flops | bytes accessed | tf_op | source)
XLA Modules:
  0.0 68.1 jit_solution(13660105652918165273)
XLA Ops:
  0.0 1.4 %copy.4.columns_ref = s32[64,16]{1,0:T(8,128)} copy(s32[64,16]{0,1:T(8,128)} %param.4) | data formatting | bytes 8192 | tf_op args[1]
  1.4 64.8 %shard_map.37 = bf16[8,4,64,64]{3,2,1,0:T(8,128)(2,1)} custom-call(s32[64]{0:T(128)} %live_ref.1, bf16[8,4,64,64]{3,2,1,0:T(8,128)(2,1)} %density_ref.1, s32[64,16]{1,0:T(8,128)} %copy.4.columns_ref), custom_call_target="tpu_custom_call" | custom-call | tf_op jit(solution)/shard_map/pallas_call | solution.py:219
  66.2 1.9 %copy.6 = bf16[8,4,64,64]{3,2,1,0:T(8,128)(2,1)} copy(bf16[8,4,64,64]{3,2,1,0:T(8,128)(2,1)} %shard_map.37) | data formatting | bytes 524288

commit v2 on v1

--- a/solution.py
+++ b/solution.py
@@ -10,7 +10,7 @@
 MESH = pl.DeviceIdType.MESH
 BF = jnp.bfloat16
 F32 = jnp.float32
-REACH = (0, 1, -1, 2, -2)
+CHUNKS = 4
 
 
 def iota(shape, dim):
@@ -43,9 +43,46 @@
     return onehot(jnp.broadcast_to(place, (512, 512)) == iota((512, 512), 1))
 
 
+class Gather:
+    def __init__(self, ref, send, recv, dom, ka):
+        flip = ka + 1 - 2 * lax.rem(ka, 2)
+        across = lax.rem(ka + 2, 4)
+
+        def copy(quarter, to, n, part):
+            rows = pl.ds(part * 128, 128)
+            return pltpu.make_async_remote_copy(
+                src_ref=ref.at[quarter, rows], dst_ref=ref.at[quarter, rows],
+                send_sem=send.at[n, part], recv_sem=recv.at[n, part],
+                device_id=(dom, to), device_id_type=MESH)
+
+        self.far = [copy(ka, across, 0, c) for c in range(CHUNKS)]
+        self.close = [copy(ka, flip, 1, c) for c in range(CHUNKS)]
+        self.passed = [copy(across, flip, 2, c) for c in range(CHUNKS)]
+
+    def start(self, part):
+        self.far[part].start()
+        self.close[part].start()
+
+    def forward(self, part):
+        self.far[part].wait_recv()
+        self.passed[part].start()
+
+    def wait_part(self, part):
+        self.close[part].wait_recv()
+        self.passed[part].wait_recv()
+
+    def wait(self):
+        for part in range(CHUNKS):
+            self.wait_part(part)
+
+    def finish(self):
+        for copy in self.far + self.close + self.passed:
+            copy.wait_send()
+
+
 def kernel(
     ndom, rows_total, live_ref, density_ref, columns_ref, out_ref,
-    a_buf, pieces, zin, win, left_in, square_in, square_own, new_pieces, yin,
+    a_buf, pieces, zin, win, left_in, square_in, new_pieces, yin,
     expand, gather, ldense, ddense, total, square_f32, mask_buf, rel_buf,
     send_a, recv_a, send_w, recv_w, send_l, recv_l, send_s, recv_s, send_n, recv_n,
 ):
@@ -58,8 +95,9 @@
         return lax.rem(ka + shift, 4)
 
     barrier = pltpu.get_barrier_semaphore()
-    for shift in REACH[1:]:
-        pl.semaphore_signal(barrier, inc=1, device_id=(near(shift), ka), device_id_type=MESH)
+    side = 1 - 2 * lax.rem(dom, 2)
+    for to in (near(2), near(-2), near(side)):
+        pl.semaphore_signal(barrier, inc=1, device_id=(to, ka), device_id_type=MESH)
     for shift in (1, 2, 3):
         pl.semaphore_signal(barrier, inc=1, device_id=(dom, peer(shift)), device_id_type=MESH)
 
@@ -73,7 +111,7 @@
         pieces[k] = packed[:, k * 128:(k + 1) * 128]
     zin[ka] = pieces[ka]
 
-    pl.semaphore_wait(barrier, 7)
+    pl.semaphore_wait(barrier, 6)
 
     def spread(src_of, dst, send, recv):
         copies = []
@@ -128,77 +166,111 @@
     win[2, 256:512, :] = mine[:, 256:512]
     left_in[ka] = win[2]
 
-    copies_w = {}
-    for n, shift in enumerate((2, -2, 1, -1)):
-        copies_w[shift] = pltpu.make_async_remote_copy(
-            src_ref=win.at[2], dst_ref=win.at[2 - shift],
-            send_sem=send_w.at[n], recv_sem=recv_w.at[n],
-            device_id=(near(shift), ka), device_id_type=MESH)
-        copies_w[shift].start()
-    copies_l = spread(lambda to: win.at[2], left_in, send_l, recv_l)
-
-    for o in (0, 1, 3, 4):
-        build(o)
+    def to_dom(src, dst, part, to, n):
+        rows = pl.ds(part * 128, 128)
+        return pltpu.make_async_remote_copy(
+            src_ref=win.at[src, rows], dst_ref=win.at[dst, rows],
+            send_sem=send_w.at[n, part], recv_sem=recv_w.at[n, part],
+            device_id=(to, ka), device_id_type=MESH)
+
+    parts = range(CHUNKS)
+    up = [to_dom(2, 0, c, near(2), 0) for c in parts]
+    down = [to_dom(2, 4, c, near(-2), 1) for c in parts]
+    beside = [to_dom(2, 2 - side, c, near(side), 2) for c in parts]
+    passed = [to_dom(2 + 2 * side, 2 + side, c, near(side), 3) for c in parts]
+    left = Gather(left_in, send_l, recv_l, dom, ka)
+    for c in parts:
+        up[c].start()
+        down[c].start()
+        left.start(c)
+        beside[c].start()
+
+    def pass_window(c):
+        up[c].wait_recv()
+        down[c].wait_recv()
+        passed[c].start()
+
+    build(0)
+    left.forward(0)
+    build(1)
+    left.forward(1)
+    pass_window(0)
+    build(3)
+    left.forward(2)
+    build(4)
+    left.forward(3)
+    pass_window(1)
     for r in range(8):
         hit = jnp.max(expand[16 + r].astype(F32), axis=0, keepdims=True)
         mask_buf[r:r + 1, :] = hit
 
     def expand_window(o):
-        def step(r, _):
-            d = exact_dot(win[o, pl.ds(pl.multiple_of(r * 64, 64), 64), :], expand[o * 8 + r])
+        for r in range(8):
+            d = exact_dot(win[o, r * 64:(r + 1) * 64, :], expand[o * 8 + r])
             for k in range(4):
                 at = pl.multiple_of(o * 512 + k * 128 + r * 16, 16)
                 ddense[pl.ds(at, 16), :] = d[k * 16:(k + 1) * 16, :]
-            return 0
-        lax.fori_loop(0, 8, step, 0)
-
-    def expand_left(src):
-        def step(r, _):
-            rows = pl.ds(pl.multiple_of(r * 64, 64), 64)
-            x = jnp.concatenate([src[k, rows, :] for k in range(4)], axis=0)
-            d = exact_dot(x, expand[16 + r])
-            for k in range(4):
-                for o in range(5):
-                    ldense[rows, o * 512 + k * 128:o * 512 + (k + 1) * 128] = (
-                        d[k * 64:(k + 1) * 64, o * 128:(o + 1) * 128])
-            return 0
-        lax.fori_loop(0, 8, step, 0)
+
+    def expand_left(src, r):
+        rows = slice(r * 64, (r + 1) * 64)
+        x = jnp.concatenate([src[k, rows, :] for k in range(4)], axis=0)
+        d = exact_dot(x, expand[16 + r])
+        for k in range(4):
+            for o in range(5):
+                ldense[rows, o * 512 + k * 128:o * 512 + (k + 1) * 128] = (
+                    d[k * 64:(k + 1) * 64, o * 128:(o + 1) * 128])
+
+    def product(o):
+        at = pl.ds(pl.multiple_of(o * 512, 512), 512)
+        return dot(ldense[:, at], ddense[at, :])
 
     expand_window(2)
-    for copy in copies_l:
+    left.wait()
+    for r in range(8):
+        expand_left(left_in, r)
+    pass_window(2)
+    square_f32[...] = product(2)
+    for copy in beside:
         copy.wait_recv()
-    expand_left(left_in)
-    square_f32[...] = dot(ldense[:, 1024:1536], ddense[1024:1536, :])
-    for shift in (1, -1, 2, -2):
-        o = 2 - shift
-        copies_w[shift].wait_recv()
+    expand_window(2 + side)
+    square_f32[...] += product(2 + side)
+    pass_window(3)
+    for o in (0, 4):
         expand_window(o)
-        square_f32[...] += dot(ldense[:, o * 512:(o + 1) * 512], ddense[o * 512:(o + 1) * 512, :])
+        square_f32[...] += product(o)
+    for copy in passed:
+        copy.wait_recv()
+    expand_window(2 - side)
+    square_f32[...] += product(2 - side)
 
     def pick(value, r):
         kept = jnp.where(mask_buf[pl.ds(r, 1), :] > 0.5, value, F32(0))
         return exact_dot(kept.astype(BF), gather[r])
 
-    for r in range(8):
-        rows = slice(r * 64, (r + 1) * 64)
-        square_own[rows, :] = pick(square_f32[rows, :], r)
-    square_in[ka] = square_own[...]
-    copies_s = spread(lambda to: square_own, square_in, send_s, recv_s)
-    for copy in copies_s:
-        copy.wait_recv()
-    expand_left(square_in)
+    squares = Gather(square_in, send_s, recv_s, dom, ka)
+    for c in parts:
+        for r in (2 * c, 2 * c + 1):
+            rows = slice(r * 64, (r + 1) * 64)
+            square_in[ka, rows, :] = pick(square_f32[rows, :], r)
+        squares.start(c)
+    for c in parts:
+        squares.forward(c)
+    turn, back = permutation("hku", "khu"), permutation("khu", "huk")
+    for c in parts:
+        squares.wait_part(c)
+        expand_left(square_in, 2 * c)
+        expand_left(square_in, 2 * c + 1)
     total[...] = 3.0 * square_f32[...] - 2.0 * dot(ldense[...], ddense[...])
     news = []
     for r in range(8):
         news.append(pick(total[r * 64:(r + 1) * 64, :], r))
     new = jnp.concatenate(
         [jnp.concatenate(news[:4], axis=0), jnp.concatenate(news[4:], axis=0)], axis=1)
-    packed = exact_dot(new, permutation("hku", "khu"))
+    packed = exact_dot(new, turn)
     for k in range(4):
         new_pieces[k] = packed[:, k * 128:(k + 1) * 128]
     yin[ka] = new_pieces[ka]
     copies_n = spread(lambda to: new_pieces.at[to], yin, send_n, recv_n)
-    back = permutation("khu", "huk")
     for copy in copies_n:
         copy.wait_recv()
     y = exact_dot(jnp.concatenate([yin[k] for k in range(4)], axis=1), back)
@@ -207,9 +279,11 @@
             for u in range(4):
                 at = (h * 4 + u) * 64
                 out_ref[h * 4 + i, u] = y[i * 64:(i + 1) * 64, at:at + 64]
-    for copies in (copies_a, copies_l, copies_s, copies_n, list(copies_w.values())):
+    for copies in (copies_a, copies_n, up, down, beside, passed):
         for copy in copies:
             copy.wait_send()
+    left.finish()
+    squares.finish()
 
 
 def shards(density, columns, live):
@@ -232,7 +306,6 @@
             vmem((5, 512, 256), BF),
             vmem((4, 512, 256), BF),
             vmem((4, 512, 256), BF),
-            vmem((512, 256), BF),
             vmem((4, 256, 128), BF),
             vmem((4, 256, 128), BF),
             vmem((40, 256, 640), BF),
@@ -243,8 +316,9 @@
             vmem((512, 640), F32),
             vmem((8, 640), F32),
             vmem((40, 16), F32),
-            dma((3,)), dma((3,)), dma((4,)), dma((4,)), dma((3,)), dma((3,)),
-            dma((3,)), dma((3,)), dma((3,)), dma((3,)),
+            dma((3,)), dma((3,)), dma((4, CHUNKS)), dma((4, CHUNKS)),
+            dma((3, CHUNKS)), dma((3, CHUNKS)), dma((3, CHUNKS)), dma((3, CHUNKS)),
+            dma((3,)), dma((3,)),
         ],
         compiler_params=pltpu.CompilerParams(
             collective_id=0, has_side_effects=True, vmem_limit_bytes=56 * 1024 * 1024),

time: 68.3 us -> 49.9 us (0.73)
  Pallas kernels: 64.8 us -> 46.3 us
    pallas_call x1, Pallas kernels: 64.8 us -> 46.3 us  [shards(): pl.pallas_call(functools.partial(kernel, lax.axis_size('dom'), rows_total...]
where the time goes in v2:
time: 49.9 us; the launch traced here: 49.6 us
  Pallas kernels  46.3 us (93%)
  local copies, waits for them, and re-layouts  3.26 us (7%)
    pallas_call x1, Pallas kernels, shards(): pl.pallas_call(functools.partial(kernel, lax.axis_size('dom'), rows_total...  46.3 us
    unnamed x2, local copies, waits for them, and re-layouts  3.26 us

profile of v2, /device:TPU:0, one launch (start us, length us, event | category | flops | bytes accessed | tf_op | source)
XLA Modules:
  0.0 49.6 jit_solution(7949239479311711726)
XLA Ops:
  0.0 1.4 %copy.4.columns_ref = s32[64,16]{1,0:T(8,128)} copy(s32[64,16]{0,1:T(8,128)} %param.4) | data formatting | bytes 8192 | tf_op args[1]
  1.4 46.3 %shard_map.37 = bf16[8,4,64,64]{3,2,1,0:T(8,128)(2,1)} custom-call(s32[64]{0:T(128)} %live_ref.1, bf16[8,4,64,64]{3,2,1,0:T(8,128)(2,1)} %density_ref.1, s32[64,16]{1,0:T(8,128)} %copy.4.columns_ref), custom_call_target="tpu_custom_call" | custom-call | tf_op jit(solution)/shard_map/pallas_call | solution.py:293
  47.8 1.9 %copy.6 = bf16[8,4,64,64]{3,2,1,0:T(8,128)(2,1)} copy(bf16[8,4,64,64]{3,2,1,0:T(8,128)(2,1)} %shard_map.37) | data formatting | bytes 524288
